TPU v7x, 256 devices: a whole 4x4x8 slice. The times are simulated.
256 devices in a mesh: dp: 8 (over z_lo, core), row: 4 (over x), col: 8 (over z_hi, y).
Axes of the slice: x: 4, y: 4, z: 8 (z_hi: 2, z_lo: 4; z = z_hi * 4 + z_lo), core: 2. Of those that a mesh axis runs over, the one named last changes fastest.
Arguments:
- inputs: bfloat16 [1024, 8192], P('dp', ('row', 'col')), may hold values from -6 to 6
- grad_out: bfloat16 [1024, 8192], P('dp', ('row', 'col')), may hold values from -6 to 6
- up_blocks: bfloat16 [4096, 128, 128], P(('row', 'col')), may hold values from -0.125 to 0.125
- up_index: int32 [4096], P(('row', 'col')), may hold values from 0 to 63, as said below
- down_blocks: bfloat16 [4096, 128, 128], P(('row', 'col')), may hold values from -0.0625 to 0.0625
- down_index: int32 [4096], P(('row', 'col')), may hold values from 0 to 255, as said below
Outputs:
- outputs: bfloat16 [1024, 8192], P('dp', ('row', 'col'))
- grad_in: bfloat16 [1024, 8192], P('dp', ('row', 'col'))
- grad_up: float32 [4096, 128, 128], P(('row', 'col'), 'dp')
- grad_down: float32 [4096, 128, 128], P(('row', 'col'), 'dp')
Inputs may be any that keep to these rules, and one draw needn't show every extreme that they name: `up_index`: for each row tile r and column block j, the 4 entries of run (r, j) name distinct row blocks of row tile r. Within row tile r and column tile c they are r * 16 + ((j mod 16) XOR m XOR o), m over a set of 4 values closed under XOR, o fixed for the tile. `down_index`: for each row tile r, column tile c and feature block i of row tile r, the 8 entries name distinct hidden-unit blocks of column tile c: c * 32 + ((i mod 32) XOR m XOR o), m over a set of 8 values closed under XOR, o fixed for the tile.
All inputs are finite; a program needn't handle non-finite values.
Results may differ from a plain program's by a relative error of at most 0.024.
Values may be sent and summed in bfloat16 or wider, within the bound.
No kernel may reach another device: no remote copies, remote signals or barrier semaphores. Data moves between devices by JAX's collectives and lax.ppermute only.
A program may use at most 128 MiB of HBM per device.

v0:
```python
import jax
import jax.numpy as jnp
from jax import lax
from jax.sharding import PartitionSpec as P

KB = 4
KB2 = 8


gelu_scale = 0.7978845608028654
cubic_term = 0.044715


def gelu_value(values):
    inside = gelu_scale * (values + cubic_term * values * values * values)
    return 0.5 * values * (1.0 + jnp.tanh(inside))


def gelu_slope(values):
    tangent = jnp.tanh(gelu_scale * (values + cubic_term * values * values * values))
    return 0.5 * (1.0 + tangent) + 0.5 * values * (1.0 - tangent * tangent) * gelu_scale * (
        1.0 + 3.0 * cubic_term * values * values
    )


def pick_blocks(split_pieces, where):
    return jnp.take(split_pieces, where, axis=1)


def local(inputs, grad_out, up_blocks, up_index, down_blocks, down_index):
    block_size = up_blocks.shape[1]
    input_panel, grad_panel = (
        lax.all_gather(inputs, "col", axis=1, tiled=True),
        lax.all_gather(grad_out, "col", axis=1, tiled=True),
    )
    token_count = input_panel.shape[0]
    row_blocks = input_panel.shape[1] // block_size
    col_blocks = up_blocks.shape[0] // KB
    up_local = (up_index - lax.axis_index("row") * row_blocks).reshape(col_blocks, KB)
    down_local = (down_index - lax.axis_index("col") * col_blocks).reshape(row_blocks, KB2)
    up_flat = up_local.reshape(-1)
    down_flat = down_local.reshape(-1)
    up_tiles = up_blocks.reshape(col_blocks, KB, block_size, block_size)
    down_block_tiles = down_blocks.reshape(row_blocks, KB2, block_size, block_size)
    height = input_panel.shape[0]
    split_pieces = input_panel.reshape(height, row_blocks, block_size)
    picked = pick_blocks(split_pieces, up_local)
    running = jnp.einsum("njkd,jkde->nje", picked, up_tiles, preferred_element_type=jnp.float32)
    hidden = lax.psum(
        running.reshape(height, col_blocks * block_size).astype(jnp.bfloat16), "row"
    ).astype(jnp.float32)
    active = gelu_value(hidden).astype(jnp.bfloat16)
    height = active.shape[0]
    split_pieces = active.reshape(height, col_blocks, block_size)
    picked = pick_blocks(split_pieces, down_local)
    running = jnp.einsum(
        "ftkj,tkjo->fto", picked, down_block_tiles, preferred_element_type=jnp.float32
    )
    outputs = lax.psum_scatter(
        running.reshape(height, row_blocks * block_size).astype(jnp.bfloat16),
        "col",
        scatter_dimension=1,
        tiled=True,
    )
    height = grad_panel.shape[0]
    split_pieces = grad_panel.reshape(height, row_blocks, block_size)
    contrib = jnp.einsum(
        "ctx,tkvx->ctkv", split_pieces, down_block_tiles, preferred_element_type=jnp.float32
    )
    running = jnp.zeros((height, col_blocks, block_size), jnp.float32)
    running = running.at[:, down_flat].add(contrib.reshape(height, row_blocks * KB2, block_size))
    grad_act = lax.psum(
        running.reshape(height, col_blocks * block_size).astype(jnp.bfloat16), "row"
    ).astype(jnp.float32)
    grad_hidden = (grad_act * gelu_slope(hidden)).astype(jnp.bfloat16)
    height = grad_hidden.shape[0]
    split_pieces = grad_hidden.reshape(height, col_blocks, block_size)
    contrib = jnp.einsum(
        "nje,jkde->njkd", split_pieces, up_tiles, preferred_element_type=jnp.float32
    )
    running = jnp.zeros((height, row_blocks, block_size), jnp.float32)
    running = running.at[:, up_flat].add(contrib.reshape(height, col_blocks * KB, block_size))
    grad_in = lax.psum_scatter(
        running.reshape(height, row_blocks * block_size).astype(jnp.bfloat16),
        "col",
        scatter_dimension=1,
        tiled=True,
    )
    act_pieces = active.reshape(token_count, col_blocks, block_size)
    grad_pieces = grad_panel.reshape(token_count, row_blocks, block_size)
    picked = pick_blocks(act_pieces, down_local)
    result = jnp.einsum("amqk,amf->mqkf", picked, grad_pieces, preferred_element_type=jnp.float32)
    input_pieces = input_panel.reshape(token_count, row_blocks, block_size)
    hidden_pieces = grad_hidden.reshape(token_count, col_blocks, block_size)
    picked = pick_blocks(input_pieces, up_local)
    up_result = jnp.einsum(
        "njkd,nje->jkde", picked, hidden_pieces, preferred_element_type=jnp.float32
    )
    grad_up = lax.psum_scatter(
        up_result.reshape(col_blocks * KB, block_size, block_size).astype(jnp.bfloat16),
        "dp",
        scatter_dimension=1,
        tiled=True,
    ).astype(jnp.float32)
    grad_down = lax.psum_scatter(
        result.reshape(row_blocks * KB2, block_size, block_size).astype(jnp.bfloat16),
        "dp",
        scatter_dimension=1,
        tiled=True,
    ).astype(jnp.float32)
    return (outputs, grad_in, grad_up, grad_down)


def solution(mesh):
    placed = (
        P("dp", ("row", "col")),
        P("dp", ("row", "col")),
        P(("row", "col"), None, None),
        P(("row", "col")),
        P(("row", "col"), None, None),
        P(("row", "col")),
    )
    return jax.shard_map(
        local,
        mesh=mesh,
        in_specs=placed,
        out_specs=(
            P("dp", ("row", "col")),
            P("dp", ("row", "col")),
            P(("row", "col"), "dp", None),
            P(("row", "col"), "dp", None),
        ),
        check_vma=False,
    )
```

profile of v0, /device:TPU:32, one launch (start us, length us, event | category | flops | bytes accessed | tf_op | source)
XLA Modules:
  0.0 532.1 jit_solution(2259402550307158597)
XLA Ops:
  9.1 46.6 %all_gather.6 = bf16[128,2048]{0,1:T(8,128)(2,1)S(1)} all-gather(bf16[128,256]{0,1:T(8,128)(2,1)S(1)} %copy.32), channel_id=1, replica_groups=mesh['dp'=8,'row'=4,'col'=8] {'col'}, dimensions={1}, use_global_device_ids=true | all-gather | bytes 589824 | tf_op jit(solution)/shard_map/all_gather | solution.py:33
  56.0 3.0 gather_fusion
  59.0 6.5 %copy.34 = bf16[32,4,128,128]{2,3,1,0:T(8,128)(2,1)} copy(bf16[32,4,128,128]{3,2,1,0:T(8,128)(2,1)} %bitcast.77) | data formatting | bytes 8388608 | tf_op jit(solution)/shard_map/jit(_take)/gather | solution.py:27
  65.6 45.8 %all_gather.7 = bf16[128,2048]{0,1:T(8,128)(2,1)S(1)} all-gather(bf16[128,256]{0,1:T(8,128)(2,1)S(1)} %copy.40), channel_id=1, replica_groups=mesh['dp'=8,'row'=4,'col'=8] {'col'}, dimensions={1}, use_global_device_ids=true | all-gather | bytes 589824 | tf_op jit(solution)/shard_map/all_gather | solution.py:34
  111.4 6.8 %fusion.41 = f32[16,8,128,128]{3,2,1,0:T(8,128)} fusion(bf16[16,8,128,128]{3,2,1,0:T(8,128)(2,1)} %bitcast.78, bf16[128,16,128,1]{0,2,3,1:T(8,128)(2,1)S(1)} %bitcast.89), kind=kOutput, calls=%fused_computation.55 | convolution fusion | flops 536870912 | bytes 13107200 | tf_op jit(solution)/shard_map/ctx,tkvx->ctkv/dot_general | solution.py:67
  118.3 9.0 %copy.42 = f32[128,128,128]{2,0,1:T(8,128)} copy(f32[128,128,128]{0,2,1:T(8,128)} %bitcast.75) | data formatting | bytes 16777216 | tf_op jit(solution)/shard_map/reshape | solution.py:71
  127.5 17.0 %scatter_fusion = f32[128,32,128]{2,0,1:T(8,128)S(1)} fusion(f32[128,32,128]{2,0,1:T(8,128)S(1)} %broadcast_in_dim.32, s32[128]{0:T(128)S(1)} %get-tuple-element.18, f32[128,128,128]{2,1,0:T(8,128)} %bitcast.73), kind=kCustom, calls=%fused_computation.2 | custom fusion | flops 2097152 | bytes 25166336 | tf_op jit(solution)/shard_map/scatter-add | solution.py:71
  146.0 6.1 %bitcast_convert_fusion = bf16[32,128,128]{1,2,0:T(8,128)(2,1)} fusion(bf16[32,4,128,128]{3,2,1,0:T(8,128)(2,1)} %bitcast.82, bf16[32,4,128,128]{2,3,1,0:T(8,128)(2,1)} %copy.34, pred[32,4]{1,0:T(8,128)(4,1)S(1)} %compare_and_fusion), kind=kOutput, calls=%fused_computation.34 | convolution fusion | flops 539492352 | bytes 9437312 | tf_op jit(solution)/shard_map/njkd,jkde->nje/dot_general | solution.py:48
  152.1 64.0 %all-reduce.3.cloned.1.call-done = (bf16[128,4096]{0,1:T(8,128)(2,1)}, bf16[128,4096]{0,1:T(8,128)(2,1)}) async-done(((bf16[128,4096]{0,1:T(8,128)(2,1)}, bf16[128,4096]{0,1:T(8,128)(2,1)}), (bf16[128,4096]{0,1:T(8,128)(2,1)}, bf16[128,4096]{0,1:T(8,128)(2,1)})) %all-reduce.3.cloned.1.call-update) | async-done | bytes 2097168 | tf_op jit(solution)/shard_map/psum | solution.py:49
  216.1 3.3 fusion.21
  219.4 4.5 fusion.42
  224.1 17.0 %scatter_fusion.1 = f32[128,16,128]{2,0,1:T(8,128)S(1)} fusion(f32[128,16,128]{2,0,1:T(8,128)S(1)} %broadcast_in_dim.30, s32[128]{0:T(128)S(1)} %get-tuple-element.16, f32[128,128,128]{2,1,0:T(8,128)} %bitcast.74), kind=kCustom, calls=%fused_computation.3 | custom fusion | flops 2097152 | bytes 25166336 | tf_op jit(solution)/shard_map/scatter-add | solution.py:82
  242.0 2.0 copy.45
  244.3 5.4 %fusion.8 = bf16[32,4,128,128]{3,2,1,0:T(8,128)(2,1)} fusion(bf16[128,32,128,1]{0,2,3,1:T(8,128)(2,1)S(1)} %bitcast.88, bf16[32,4,128,128]{2,3,1,0:T(8,128)(2,1)} %copy.34, pred[32,4]{1,0:T(8,128)(4,1)S(1)} %compare_and_fusion), kind=kOutput, calls=%fused_computation.21 | convolution fusion | flops 541065216 | bytes 9437312 | tf_op jit(solution)/shard_map/njkd,nje->jkde/dot_general | solution.py:96
  250.0 3.0 gather_fusion.1
  253.0 5.4 %fusion.11 = bf16[16,8,128,128]{3,2,1,0:T(8,128)(2,1)} fusion(bf16[128,16,128,1]{0,2,3,1:T(8,128)(2,1)S(1)} %bitcast.90, bf16[16,8,128,128]{2,3,1,0:T(8,128)(2,1)} %bitcast.80, pred[16,8]{1,0:T(8,128)(4,1)S(1)} %compare_and_fusion.1), kind=kOutput, calls=%fused_computation.22 | convolution fusion | flops 541065216 | bytes 8913024 | tf_op jit(solution)/shard_map/amqk,amf->mqkf/dot_general | solution.py:92
  258.5 5.1 fusion.34
  264.7 62.7 %reduce-scatter.7.cloned.1.call-done = bf16[128,256]{0,1:T(8,128)(2,1)} async-done(((bf16[128,2048]{0,1:T(8,128)(2,1)}), bf16[128,256]{0,1:T(8,128)(2,1)}) %reduce-scatter.7.cloned.1.call-update) | async-done | bytes 65552 | tf_op jit(solution)/shard_map/reduce_scatter | solution.py:83
  327.5 1.6 copy.48
  329.1 49.1 %reduce-scatter.9.cloned.1.call-done = bf16[128,16,128]{2,1,0:T(8,128)(2,1)} async-done(((bf16[128,128,128]{2,1,0:T(8,128)(2,1)}), bf16[128,16,128]{2,1,0:T(8,128)(2,1)}) %reduce-scatter.9.cloned.1.call-update) | async-done | bytes 524304 | tf_op jit(solution)/shard_map/reduce_scatter | solution.py:99
  378.2 2.1 convert_element_type.76
  380.2 54.5 %reduce-scatter.11.cloned.1.call-done = bf16[128,16,128]{2,1,0:T(8,128)(2,1)} async-done(((bf16[128,128,128]{2,1,0:T(8,128)(2,1)}), bf16[128,16,128]{2,1,0:T(8,128)(2,1)}) %reduce-scatter.11.cloned.1.call-update) | async-done | bytes 524304 | tf_op jit(solution)/shard_map/reduce_scatter | solution.py:105
  434.7 2.1 convert_element_type.79
  436.8 88.8 %reduce-scatter.5.cloned.1.call-done = bf16[128,256]{1,0:T(8,128)(2,1)} async-done(((bf16[128,2048]{1,0:T(8,128)(2,1)}), bf16[128,256]{1,0:T(8,128)(2,1)}) %reduce-scatter.5.cloned.1.call-update) | async-done | bytes 65552 | tf_op jit(solution)/shard_map/reduce_scatter | solution.py:59
  (41 shorter events, 6.6 us)
Async XLA Ops:
  7.2 208.9 %all-reduce.3.cloned.1.call-start = ((), (), s32[]{:S(2)}) async-start(), calls=%async_computation.8 | async-start | bytes 4194304 | tf_op jit(solution)/shard_map/psum | solution.py:49
  59.0 6.5 %copy-start.3 = (bf16[128,256]{1,0:T(8,128)(2,1)S(1)}, bf16[128,256]{1,0:T(8,128)(2,1)}, u32[]{:S(2)}) copy-start(bf16[128,256]{1,0:T(8,128)(2,1)} %param.11) | copy-start | bytes 196612
  111.4 6.8 %copy-start.1 = (bf16[128,2048]{0,1:T(8,128)(2,1)}, bf16[128,2048]{0,1:T(8,128)(2,1)S(1)}, u32[]{:S(2)}) copy-start(bf16[128,2048]{0,1:T(8,128)(2,1)S(1)} %all_gather.7) | copy-start | bytes 1572868
  118.3 9.0 %copy-start.4 = (s32[128]{0:T(128)S(1)}, s32[128]{0:T(128)}, u32[]{:S(2)}) copy-start(s32[128]{0:T(128)} %param.15) | copy-start | bytes 1540
  152.1 175.4 %reduce-scatter.7.cloned.1.call-start = ((), (), s32[]{:S(2)}) async-start(), calls=%async_computation.5 | async-start | bytes 589824 | tf_op jit(solution)/shard_map/reduce_scatter | solution.py:83
  216.1 3.3 copy-start
  244.0 134.1 %reduce-scatter.9.cloned.1.call-start = ((), (), s32[]{:S(2)}) async-start(), calls=%async_computation.6 | async-start | bytes 4718592 | tf_op jit(solution)/shard_map/reduce_scatter | solution.py:99
  249.7 185.0 %reduce-scatter.11.cloned.1.call-start = ((), (), s32[]{:S(2)}) async-start(), calls=%async_computation.7 | async-start | bytes 4718592 | tf_op jit(solution)/shard_map/reduce_scatter | solution.py:105
  250.0 3.0 copy-start.2
  258.5 267.1 %reduce-scatter.5.cloned.1.call-start = ((), (), s32[]{:S(2)}) async-start(), calls=%async_computation.4 | async-start | bytes 589824 | tf_op jit(solution)/shard_map/reduce_scatter | solution.py:59
Sparse Core Ops, SparseCore 0:
  152.2 63.8 all-reduce.2
  244.2 83.2 reduce-scatter.6
  330.0 48.0 reduce-scatter.8
  380.6 54.0 reduce-scatter.10
  439.0 86.5 reduce-scatter.4
where the time goes:
time: 535 us; the launch traced here: 532 us
  waiting for transfers between devices  319 us (60%)
  blocking collectives  92.4 us (17%)
  other arithmetic  43.3 us (8%)
  matrix products  33.4 us (6%)
  local copies, waits for them, and re-layouts  29.5 us (6%)
  between operations  13.9 us (3%)
    reduce_scatter x2, waiting for transfers between devices, local(): lax.psum_scatter(running.reshape(height, row_blocks * block_size).astype(...  152 us
    psum x1, waiting for transfers between devices, local(): lax.psum(running.reshape(height, col_blocks * block_size).astype(jnp.bflo...  64 us
    reduce_scatter x1, waiting for transfers between devices, local(): lax.psum_scatter(result.reshape(row_blocks * KB2, block_size, block_size)...  54.5 us
    reduce_scatter x1, waiting for transfers between devices, local(): lax.psum_scatter(up_result.reshape(col_blocks * KB, block_size, block_siz...  49.1 us
    all_gather x1, blocking collectives, local(): lax.all_gather(inputs, 'col', axis=1, tiled=True)  46.6 us
    all_gather x1, blocking collectives, local(): lax.all_gather(grad_out, 'col', axis=1, tiled=True)  45.8 us
    scatter-add x1, other arithmetic, local(): running.at[:, down_flat]  17 us
    scatter-add x1, other arithmetic, local(): running.at[:, up_flat]  17 us
  transfers between devices with their start and end apart: 5, of which 5 were waited for; matrix products, arithmetic and copies ran while one was open for 5% of the time, Pallas kernels for 0%

commit v1 on v0

v1 whole, which is shorter than its diff:
```python
import jax
import jax.numpy as jnp
from jax import lax
from jax.experimental import pallas as pl
from jax.experimental.pallas import tpu as pltpu
from jax.sharding import Mesh
from jax.sharding import PartitionSpec as P

KB = 4
KB2 = 8
BS = 128
ROWS = 16
COLS = 32

gelu_scale = 0.7978845608028654
cubic_term = 0.044715


def gelu_value(values):
    inside = gelu_scale * (values + cubic_term * values * values * values)
    return 0.5 * values * (1.0 + jnp.tanh(inside))


def gelu_slope(values):
    tangent = jnp.tanh(gelu_scale * (values + cubic_term * values * values * values))
    return 0.5 * (1.0 + tangent) + 0.5 * values * (1.0 - tangent * tangent) * gelu_scale * (
        1.0 + 3.0 * cubic_term * values * values
    )


SMEM = pl.BlockSpec(memory_space=pltpu.SMEM)
VMEM = pl.BlockSpec(memory_space=pltpu.VMEM)
BF = jnp.bfloat16
F32 = jnp.float32


def call(kernel, scalars, arrays, outs, scratch=(), flops=1.1e9, name=None):
    moved = sum(a.size * a.dtype.itemsize for a in arrays)
    return pl.pallas_call(
        kernel,
        out_shape=outs,
        in_specs=[SMEM] * len(scalars) + [VMEM] * len(arrays),
        out_specs=[VMEM] * len(outs),
        scratch_shapes=list(scratch),
        compiler_params=pltpu.CompilerParams(vmem_limit_bytes=28 * 2**20),
        cost_estimate=pl.CostEstimate(flops=int(flops), bytes_accessed=int(moved), transcendentals=0),
        name=name,
    )(*scalars, *arrays)


def up_kernel(order, where, x, w, *outs):
    for slot, out in enumerate(outs):

        def step(jj, carry):
            j = order[slot * 8 + jj]
            lhs = jnp.concatenate([x[where[j * KB + k]] for k in range(KB)], axis=1)
            rhs = w[pl.ds(j * KB, KB)].reshape(KB * BS, BS)
            out[jj] = jnp.dot(lhs, rhs, preferred_element_type=F32).astype(BF)
            return carry

        lax.fori_loop(0, 8, step, 0, unroll=4)


def down_kernel(order, where, a, w, *outs):
    for slot, out in enumerate(outs):

        def step(ii, carry):
            i = order[slot * 4 + ii]
            lhs = jnp.concatenate([a[where[i * KB2 + k]] for k in range(KB2)], axis=1)
            rhs = w[pl.ds(i * KB2, KB2)].reshape(KB2 * BS, BS)
            out[ii] = jnp.dot(lhs, rhs, preferred_element_type=F32).astype(BF)
            return carry

        lax.fori_loop(0, 4, step, 0, unroll=2)


def spread_kernel(runs, width, pieces, order, where, v, w, *rest):
    outs, acc = rest[:-1], rest[-1]
    acc[...] = jnp.zeros_like(acc)

    def step(loc, carry):
        run = order[loc]
        rhs = w[pl.ds(run * width, width)].reshape(width * BS, BS)
        got = lax.dot_general(v[loc], rhs, (((1,), (1,)), ((), ())), preferred_element_type=F32)
        for k in range(width):
            at = where[run * width + k]
            acc[at] = acc[at] + got[:, k * BS:(k + 1) * BS]
        return carry

    lax.fori_loop(0, runs, step, 0, unroll=2)
    for slot, out in enumerate(outs):
        out[...] = acc[slot * pieces:(slot + 1) * pieces].astype(BF)


def term_kernel(runs, width, many, spot, where, place, u0, u1, v0, v1, out, turned):
    half = place[0]

    def turn(b, carry):
        turned[b, :, :BS] = u0[b].T
        turned[b, :, BS:] = u1[b].T
        return carry

    lax.fori_loop(0, many, turn, 0, unroll=4)

    def step(n, carry):
        run = half * runs + n
        lhs = jnp.concatenate([turned[where[run * width + k]] for k in range(width)], axis=0)
        at = spot[run]
        rhs = jnp.concatenate([v0[at], v1[at]], axis=0)
        got = jnp.dot(lhs, rhs, preferred_element_type=F32).astype(BF)
        got = got.reshape(width, 4, 2, 16, BS)
        for z in range(4):
            for side in range(2):
                out[z, jnp.bitwise_xor(side, half), pl.ds(n * width, width)] = got[:, z, side]
        return carry

    lax.fori_loop(0, runs, step, 0, unroll=2)


def shift(value, axis, size, by):
    return lax.ppermute(value, axis, [(i, (i + by) % size) for i in range(size)])


def swap(value, axis):
    return lax.ppermute(value, axis, [(0, 1), (1, 0)])


def spread(own, axis):
    return jnp.concatenate([own] + [shift(own, axis, 4, -s) for s in (1, 2, 3)], axis=0)


def total(parts, axis):
    got = [shift(parts[s], axis, 4, s) for s in (1, 2, 3)]
    return sum((g.astype(F32) for g in got), parts[0].astype(F32))


def gather_features(value):
    pieces = jnp.transpose(value.reshape(BS, 2, BS), (1, 0, 2))
    return spread(jnp.concatenate([pieces, swap(pieces, "h")], axis=0), "y")


def scatter_features(parts):
    mine = total(parts, "y").reshape(2, 2, BS, BS)
    done = mine[0] + swap(mine[1].astype(BF), "h").astype(F32)
    return jnp.transpose(done.astype(BF), (1, 0, 2)).reshape(BS, 2 * BS)


def finish(terms, half):
    mine = lax.psum_scatter(terms, "z", scatter_dimension=0, tiled=True)[0]
    own, other = mine[0], swap(mine[1], "q")
    low = jnp.where(half == 0, own, other)
    high = jnp.where(half == 0, other, own)
    return jnp.concatenate([low, high], axis=0).astype(F32)


def local(inputs, grad_out, up_blocks, up_index, down_blocks, down_index):
    r, h, y, q = (lax.axis_index(a) for a in ("row", "h", "y", "q"))
    half = q.reshape(1).astype(jnp.int32)
    c = h * 4 + y

    def feature_spot(b):
        return ((b // 2 % 4 - y) % 4) * 4 + jnp.bitwise_xor(b // 8, h) * 2 + b % 2

    def feature_at(s):
        return jnp.bitwise_xor(s // 2 % 2, h) * 8 + ((s // 4 + y) % 4) * 2 + s % 2

    def hidden_spot(f):
        return ((f // 8 - r) % 4) * 8 + f % 8

    def hidden_at(s):
        return ((s // 8 + r) % 4) * 8 + s % 8

    features, units = jnp.arange(ROWS, dtype=jnp.int32), jnp.arange(COLS, dtype=jnp.int32)
    up_where = feature_spot(up_index - r * ROWS)
    down_where = hidden_spot(down_index - c * COLS)
    feature_spots, feature_order = feature_spot(features), feature_at(features)
    hidden_spots, hidden_order = hidden_spot(units), hidden_at(units)

    x = gather_features(inputs)
    g = gather_features(grad_out)
    piece = jax.ShapeDtypeStruct((8, BS, BS), BF)
    slab = jax.ShapeDtypeStruct((4, BS, BS), BF)

    up = call(up_kernel, (hidden_order, up_where), (x, up_blocks), [piece] * 4, name="up")
    hidden = total(up, "row")
    active = spread(gelu_value(hidden).astype(BF), "row")

    back = call(
        lambda *a: spread_kernel(ROWS, KB2, 8, *a), (feature_order, down_where), (g, down_blocks), [piece] * 4,
        [pltpu.VMEM((COLS, BS, BS), F32)], name="back",
    )
    grad_hidden = spread((total(back, "row") * gelu_slope(hidden)).astype(BF), "row")

    x2, g2 = swap(x, "q"), swap(g, "q")
    terms = jax.ShapeDtypeStruct((4, 2, 64, 16, BS), BF)

    (down_terms,) = call(
        lambda *a: term_kernel(8, KB2, COLS, *a), (feature_spots, down_where, half),
        (active, swap(active, "q"), g, g2), [terms], [pltpu.VMEM((COLS, BS, 2 * BS), BF)], name="down_terms",
    )
    grad_down = finish(down_terms, q)
    (up_terms,) = call(
        lambda *a: term_kernel(16, KB, ROWS, *a), (hidden_spots, up_where, half),
        (x, x2, grad_hidden, swap(grad_hidden, "q")), [terms], [pltpu.VMEM((ROWS, BS, 2 * BS), BF)], name="up_terms",
    )
    grad_up = finish(up_terms, q)

    down = call(down_kernel, (feature_order, down_where), (active, down_blocks), [slab] * 4, name="down")
    outputs = scatter_features(down)
    into = call(
        lambda *a: spread_kernel(COLS, KB, 4, *a), (hidden_order, up_where), (grad_hidden, up_blocks), [slab] * 4,
        [pltpu.VMEM((ROWS, BS, BS), F32)], name="into",
    )
    grad_in = scatter_features(into)
    return outputs, grad_in, grad_up, grad_down


def solution(mesh):
    fine = Mesh(mesh.devices.reshape(4, 2, 4, 2, 4), ("z", "q", "row", "h", "y"))
    tokens, width = ("z", "q"), ("row", "h", "y")
    placed = (
        P(tokens, width),
        P(tokens, width),
        P(width, None, None),
        P(width),
        P(width, None, None),
        P(width),
    )
    return jax.shard_map(
        local,
        mesh=fine,
        in_specs=placed,
        out_specs=(P(tokens, width), P(tokens, width), P(width, tokens, None), P(width, tokens, None)),
        check_vma=False,
    )
```

time: 535 us -> 205 us (0.38)
  the two profiles are of different devices: /device:TPU:32 before, /device:TPU:1 now
where the time goes in v1:
time: 205 us; the launch traced here: 204 us
  waiting for transfers between devices  102 us (50%)
  starting transfers between devices  44.5 us (22%)
  Pallas kernels  22.6 us (11%)
  between operations  14.4 us (7%)
  local copies, waits for them, and re-layouts  13.9 us (7%)
  other arithmetic  6.58 us (3%)
    ppermute x24, waiting for transfers between devices, shift(): lax.ppermute(value, axis, [(i, (i + by) % size) for i in range(size)])  50.4 us
    reduce_scatter x2, waiting for transfers between devices, finish(): mine = lax.psum_scatter(terms, 'z', scatter_dimension=0, tiled=True)[0]  41.6 us
    ppermute x24, starting transfers between devices, shift(): lax.ppermute(value, axis, [(i, (i + by) % size) for i in range(size)])  27.9 us
    pallas_call x6, Pallas kernels, call(): pl.pallas_call(kernel, out_shape=outs, in_specs=[SMEM] * len(scalars) + [...  22.6 us
    ppermute x10, starting transfers between devices, swap(): return lax.ppermute(value, axis, [(0, 1), (1, 0)])  16.4 us
    unnamed x22, local copies, waits for them, and re-layouts  11.4 us
    ppermute x10, waiting for transfers between devices, swap(): return lax.ppermute(value, axis, [(0, 1), (1, 0)])  10.3 us
  transfers between devices with their start and end apart: 36, of which 17 were waited for; matrix products, arithmetic and copies ran while one was open for 4% of the time, Pallas kernels for 8%

profile of v1, /device:TPU:1, one launch (start us, length us, event | category | flops | bytes accessed | tf_op | source)
XLA Modules:
  0.0 204.2 jit_solution(1901030817154856449)
XLA Ops:
  8.3 7.8 %collective-permute-start.14 = (bf16[2,128,128]{2,1,0:T(8,128)(2,1)S(1)}, bf16[2,128,128]{2,1,0:T(8,128)(2,1)S(1)}, u32[]{:S(2)}, u32[]{:S(2)}) collective-permute-start(bf16[2,128,128]{2,1,0:T(8,128)(2,1)S(1)} %bitcast.31), channel_id=1, source_target_pairs={{0,4},{4,0},{1,5},{5,1},{2,6},{6,2},{3,7},{7,3},{8,12},{12,8},{9,1... | collective-permute-start | bytes 196616 | tf_op jit(solution)/shard_map/ppermute | solution.py:125
  18.8 2.8 %collective-permute-start.15 = (bf16[4,128,128]{2,1,0:T(8,128)(2,1)S(1)}, bf16[4,128,128]{2,1,0:T(8,128)(2,1)S(1)}, u32[]{:S(2)}, u32[]{:S(2)}) collective-permute-start(bf16[4,128,128]{2,1,0:T(8,128)(2,1)S(1)} %pad_maximum_fusion.3), channel_id=1, source_target_pairs={{0,3},{1,0},{2,1},{3,2},{4,7},{5,4},{6,5},{7,6},{8,11},{9,8},{10,9... | collective-permute-start | bytes 393224 | tf_op jit(solution)/shard_map/ppermute | solution.py:121
  24.4 3.5 %collective-permute-start.1 = (bf16[4,128,128]{2,1,0:T(8,128)(2,1)S(1)}, bf16[4,128,128]{2,1,0:T(8,128)(2,1)S(1)}, u32[]{:S(2)}, u32[]{:S(2)}) collective-permute-start(bf16[4,128,128]{2,1,0:T(8,128)(2,1)S(1)} %pad_maximum_fusion.2), channel_id=1, source_target_pairs={{0,3},{1,0},{2,1},{3,2},{4,7},{5,4},{6,5},{7,6},{8,11},{9,8},{10,9... | collective-permute-start | bytes 393224 | tf_op jit(solution)/shard_map/ppermute | solution.py:121
  32.7 3.3 %back.1 = (bf16[8,128,128]{2,1,0:T(8,128)(2,1)S(1)}, bf16[8,128,128]{2,1,0:T(8,128)(2,1)S(1)}, bf16[8,128,128]{2,1,0:T(8,128)(2,1)S(1)}, bf16[8,128,128]{2,1,0:T(8,128)(2,1)S(1)}) custom-call(s32[16]{0:T(128)S(1)} %fusion.17.order.a_0_, s32[128]{0:T(128)S(1)} %fusion.11.where.a_1_, bf16[16,128,128]{2,1,0:T(8,128)(2,1)S(1)} %constant_dynamic-update-slice_fusion.5.a_2_.a_5_, ...), custom_call_target="tpu_custom_call" | custom-call | flops 1100000000 | bytes 4718592 | tf_op jit(solution)/shard_map/back/pallas_call | solution.py:39
  36.0 2.5 %collective-permute-start.20 = (bf16[8,128,128]{2,1,0:T(8,128)(2,1)S(1)}, bf16[8,128,128]{2,1,0:T(8,128)(2,1)S(1)}, u32[]{:S(2)}, u32[]{:S(2)}) collective-permute-start(bf16[8,128,128]{2,1,0:T(8,128)(2,1)S(1)} %get-tuple-element.31), channel_id=1, source_target_pairs={{0,24},{8,0},{16,8},{24,16},{1,25},{9,1},{17,9},{25,17},{2,26},{10... | collective-permute-start | bytes 786440 | tf_op jit(solution)/shard_map/ppermute | solution.py:121
  39.8 2.9 %up.1 = (bf16[8,128,128]{2,1,0:T(8,128)(2,1)S(1)}, bf16[8,128,128]{2,1,0:T(8,128)(2,1)S(1)}, bf16[8,128,128]{2,1,0:T(8,128)(2,1)S(1)}, bf16[8,128,128]{2,1,0:T(8,128)(2,1)S(1)}) custom-call(s32[32]{0:T(128)S(1)} %fusion.22.order.a_0_, s32[128]{0:T(128)S(1)} %fusion.12.where.a_1_, bf16[16,128,128]{2,1,0:T(8,128)(2,1)S(1)} %constant_dynamic-update-slice_fusion.x.a_3_, ...), custom_call_target="tpu_custom_call" | custom-call | flops 1100000000 | bytes 4718592 | tf_op jit(solution)/shard_map/up/pallas_call | solution.py:39
  46.3 9.6 %collective-permute-done.18 = bf16[8,128,128]{2,1,0:T(8,128)(2,1)S(1)} collective-permute-done((bf16[8,128,128]{2,1,0:T(8,128)(2,1)S(1)}, bf16[8,128,128]{2,1,0:T(8,128)(2,1)S(1)}, u32[]{:S(2)}, u32[]{:S(2)}) %collective-permute-start.18) | collective-permute-done | bytes 262176 | tf_op jit(solution)/shard_map/ppermute | solution.py:121
  57.6 7.4 %collective-permute-done.4 = bf16[8,128,128]{2,1,0:T(8,128)(2,1)S(1)} collective-permute-done((bf16[8,128,128]{2,1,0:T(8,128)(2,1)S(1)}, bf16[8,128,128]{2,1,0:T(8,128)(2,1)S(1)}, u32[]{:S(2)}, u32[]{:S(2)}) %collective-permute-start.4) | collective-permute-done | bytes 262176 | tf_op jit(solution)/shard_map/ppermute | solution.py:121
  68.5 11.4 %collective-permute-done.23 = bf16[8,128,128]{2,1,0:T(8,128)(2,1)S(1)} collective-permute-done((bf16[8,128,128]{2,1,0:T(8,128)(2,1)S(1)}, bf16[8,128,128]{2,1,0:T(8,128)(2,1)S(1)}, u32[]{:S(2)}, u32[]{:S(2)}) %collective-permute-start.23) | collective-permute-done | bytes 262176 | tf_op jit(solution)/shard_map/ppermute | solution.py:121
  82.3 2.9 %collective-permute-done.28.a_4_ = bf16[16,128,128]{2,1,0:T(8,128)(2,1)S(1)} collective-permute-done((bf16[16,128,128]{2,1,0:T(8,128)(2,1)S(1)}, bf16[16,128,128]{2,1,0:T(8,128)(2,1)S(1)}, u32[]{:S(2)}, u32[]{:S(2)}) %collective-permute-start.28) | collective-permute-done | bytes 524320 | tf_op jit(solution)/shard_map/ppermute | solution.py:125
  85.2 5.5 %up_terms.1 = bf16[4,2,64,16,128]{4,3,2,1,0:T(8,128)(2,1)} custom-call(s32[32]{0:T(128)S(1)} %fusion.27.a_0_, s32[128]{0:T(128)S(1)} %fusion.12.where.a_1_, s32[1]{0:T(128)} %bitcast.8.a_2_, bf16[16,128,128]{2,1,0:T(8,128)(2,1)S(1)} %constant_dynamic-update-slice_fusion.x.a_3_, bf16[16,128,128]{2,1,0:T(8,128)(2,1)S(1)} %collective-permute-done.28.a_4_, ...), custom_call_target="tpu_custom_call" | custom-call | flops 1100000000 | bytes 3145728 | tf_op jit(solution)/shard_map/up_terms/pallas_call | solution.py:39
  90.9 3.3 %collective-permute-start.8 = (bf16[8,128,128]{2,1,0:T(8,128)(2,1)S(1)}, bf16[8,128,128]{2,1,0:T(8,128)(2,1)S(1)}, u32[]{:S(2)}, u32[]{:S(2)}) collective-permute-start(bf16[8,128,128]{2,1,0:T(8,128)(2,1)S(1)} %get-tuple-element.41), channel_id=1, source_target_pairs={{0,16},{8,24},{16,0},{24,8},{1,17},{9,25},{17,1},{25,9},{2,18},{10... | collective-permute-start | bytes 786440 | tf_op jit(solution)/shard_map/ppermute | solution.py:121
  94.1 5.5 %collective-permute-done.9 = bf16[8,128,128]{2,1,0:T(8,128)(2,1)S(1)} collective-permute-done((bf16[8,128,128]{2,1,0:T(8,128)(2,1)S(1)}, bf16[8,128,128]{2,1,0:T(8,128)(2,1)S(1)}, u32[]{:S(2)}, u32[]{:S(2)}) %collective-permute-start.9) | collective-permute-done | bytes 262176 | tf_op jit(solution)/shard_map/ppermute | solution.py:121
  99.6 6.2 %collective-permute-done.8 = bf16[8,128,128]{2,1,0:T(8,128)(2,1)S(1)} collective-permute-done((bf16[8,128,128]{2,1,0:T(8,128)(2,1)S(1)}, bf16[8,128,128]{2,1,0:T(8,128)(2,1)S(1)}, u32[]{:S(2)}, u32[]{:S(2)}) %collective-permute-start.8) | collective-permute-done | bytes 262176 | tf_op jit(solution)/shard_map/ppermute | solution.py:121
  107.4 2.9 %collective-permute-done.32.a_6_ = bf16[16,128,128]{2,1,0:T(8,128)(2,1)S(1)} collective-permute-done((bf16[16,128,128]{2,1,0:T(8,128)(2,1)S(1)}, bf16[16,128,128]{2,1,0:T(8,128)(2,1)S(1)}, u32[]{:S(2)}, u32[]{:S(2)}) %collective-permute-start.32) | collective-permute-done | bytes 524320 | tf_op jit(solution)/shard_map/ppermute | solution.py:125
  110.3 3.3 %down_terms.1 = bf16[4,2,64,16,128]{4,3,2,1,0:T(8,128)(2,1)S(1)} custom-call(s32[16]{0:T(128)S(1)} %fusion.31.a_0_, s32[128]{0:T(128)S(1)} %fusion.11.where.a_1_, s32[1]{0:T(128)} %bitcast.8.a_2_, bf16[32,128,128]{2,1,0:T(8,128)(2,1)S(1)} %pad_maximum_fusion.a.a_3_, bf16[32,128,128]{2,1,0:T(8,128)(2,1)S(1)} %collective-permute-done.31.a_4_, ...), custom_call_target="tpu_custom_call" | custom-call | flops 1100000000 | bytes 3145728 | tf_op jit(solution)/shard_map/down_terms/pallas_call | solution.py:39
  117.2 2.9 %down.1 = (bf16[4,128,128]{2,1,0:T(8,128)(2,1)S(1)}, bf16[4,128,128]{2,1,0:T(8,128)(2,1)S(1)}, bf16[4,128,128]{2,1,0:T(8,128)(2,1)S(1)}, bf16[4,128,128]{2,1,0:T(8,128)(2,1)S(1)}) custom-call(s32[16]{0:T(128)S(1)} %fusion.17.order.a_0_, s32[128]{0:T(128)S(1)} %fusion.11.where.a_1_, bf16[32,128,128]{2,1,0:T(8,128)(2,1)S(1)} %pad_maximum_fusion.a.a_3_, ...), custom_call_target="tpu_custom_call" | custom-call | flops 1100000000 | bytes 5242880 | tf_op jit(solution)/shard_map/down/pallas_call | solution.py:39
  124.2 4.7 %into.1 = (bf16[4,128,128]{2,1,0:T(8,128)(2,1)S(1)}, bf16[4,128,128]{2,1,0:T(8,128)(2,1)S(1)}, bf16[4,128,128]{2,1,0:T(8,128)(2,1)S(1)}, bf16[4,128,128]{2,1,0:T(8,128)(2,1)S(1)}) custom-call(s32[32]{0:T(128)S(1)} %fusion.22.order.a_0_, s32[128]{0:T(128)S(1)} %fusion.12.where.a_1_, bf16[32,128,128]{2,1,0:T(8,128)(2,1)S(1)} %pad_maximum_fusion.1.a_2_.a_5_, ...), custom_call_target="tpu_custom_call" | custom-call | flops 1100000000 | bytes 5242880 | tf_op jit(solution)/shard_map/into/pallas_call | solution.py:39
  128.8 3.0 %collective-permute-start.26 = (bf16[4,128,128]{2,1,0:T(8,128)(2,1)S(1)}, bf16[4,128,128]{2,1,0:T(8,128)(2,1)S(1)}, u32[]{:S(2)}, u32[]{:S(2)}) collective-permute-start(bf16[4,128,128]{2,1,0:T(8,128)(2,1)S(1)} %get-tuple-element.35), channel_id=1, source_target_pairs={{0,3},{1,0},{2,1},{3,2},{4,7},{5,4},{6,5},{7,6},{8,11},{9,8},{10,9... | collective-permute-start | bytes 393224 | tf_op jit(solution)/shard_map/ppermute | solution.py:121
  134.2 3.0 %collective-permute-done.25 = bf16[4,128,128]{2,1,0:T(8,128)(2,1)S(1)} collective-permute-done((bf16[4,128,128]{2,1,0:T(8,128)(2,1)S(1)}, bf16[4,128,128]{2,1,0:T(8,128)(2,1)S(1)}, u32[]{:S(2)}, u32[]{:S(2)}) %collective-permute-start.25) | collective-permute-done | bytes 131104 | tf_op jit(solution)/shard_map/ppermute | solution.py:121
  137.2 3.6 %collective-permute-done.24 = bf16[4,128,128]{2,1,0:T(8,128)(2,1)S(1)} collective-permute-done((bf16[4,128,128]{2,1,0:T(8,128)(2,1)S(1)}, bf16[4,128,128]{2,1,0:T(8,128)(2,1)S(1)}, u32[]{:S(2)}, u32[]{:S(2)}) %collective-permute-start.24) | collective-permute-done | bytes 131104 | tf_op jit(solution)/shard_map/ppermute | solution.py:121
  142.0 3.2 %collective-permute-start.30 = (bf16[64,16,128]{2,1,0:T(8,128)(2,1)S(1)}, bf16[64,16,128]{2,1,0:T(8,128)(2,1)S(1)}, u32[]{:S(2)}, u32[]{:S(2)}) collective-permute-start(bf16[64,16,128]{2,1,0:T(8,128)(2,1)S(1)} %slice_bitcast_fusion.2), channel_id=1, source_target_pairs={{0,32},{32,0},{1,33},{33,1},{2,34},{34,2},{3,35},{35,3},{4,36},{36... | collective-permute-start | bytes 786440 | tf_op jit(solution)/shard_map/ppermute | solution.py:125
  145.3 2.7 %collective-permute-done.27 = bf16[2,128,128]{2,1,0:T(8,128)(2,1)S(1)} collective-permute-done((bf16[2,128,128]{2,1,0:T(8,128)(2,1)S(1)}, bf16[2,128,128]{2,1,0:T(8,128)(2,1)S(1)}, u32[]{:S(2)}, u32[]{:S(2)}) %collective-permute-start.27) | collective-permute-done | bytes 65568 | tf_op jit(solution)/shard_map/ppermute | solution.py:125
  149.8 41.6 %reduce-scatter.5.cloned.1.call-done = bf16[1,2,64,16,128]{4,3,2,1,0:T(8,128)(2,1)} async-done(((bf16[4,2,64,16,128]{4,3,2,1,0:T(8,128)(2,1)}), bf16[1,2,64,16,128]{4,3,2,1,0:T(8,128)(2,1)}) %reduce-scatter.5.cloned.1.call-update) | async-done | bytes 524304 | tf_op jit(solution)/shard_map/reduce_scatter | solution.py:149
  (107 shorter events, 44.2 us)
Async XLA Ops:
  7.2 133.9 %reduce-scatter.3.cloned.1.call-start = ((), (), s32[]{:S(2)}) async-start(), calls=%async_computation.2 | async-start | bytes 2621440 | tf_op jit(solution)/shard_map/reduce_scatter | solution.py:149
  8.3 10.5 %collective-permute-start.14 = (bf16[2,128,128]{2,1,0:T(8,128)(2,1)S(1)}, bf16[2,128,128]{2,1,0:T(8,128)(2,1)S(1)}, u32[]{:S(2)}, u32[]{:S(2)}) collective-permute-start(bf16[2,128,128]{2,1,0:T(8,128)(2,1)S(1)} %bitcast.31), channel_id=1, source_target_pairs={{0,4},{4,0},{1,5},{5,1},{2,6},{6,2},{3,7},{7,3},{8,12},{12,8},{9,1... | collective-permute-start | bytes 196616 | tf_op jit(solution)/shard_map/ppermute | solution.py:125
  18.8 9.5 %collective-permute-start.15 = (bf16[4,128,128]{2,1,0:T(8,128)(2,1)S(1)}, bf16[4,128,128]{2,1,0:T(8,128)(2,1)S(1)}, u32[]{:S(2)}, u32[]{:S(2)}) collective-permute-start(bf16[4,128,128]{2,1,0:T(8,128)(2,1)S(1)} %pad_maximum_fusion.3), channel_id=1, source_target_pairs={{0,3},{1,0},{2,1},{3,2},{4,7},{5,4},{6,5},{7,6},{8,11},{9,8},{10,9... | collective-permute-start | bytes 393224 | tf_op jit(solution)/shard_map/ppermute | solution.py:121
  21.9 8.5 %collective-permute-start.17 = (bf16[4,128,128]{2,1,0:T(8,128)(2,1)S(1)}, bf16[4,128,128]{2,1,0:T(8,128)(2,1)S(1)}, u32[]{:S(2)}, u32[]{:S(2)}) collective-permute-start(bf16[4,128,128]{2,1,0:T(8,128)(2,1)S(1)} %pad_maximum_fusion.3), channel_id=1, source_target_pairs={{0,1},{1,2},{2,3},{3,0},{4,5},{5,6},{6,7},{7,4},{8,9},{9,10},{10,1... | collective-permute-start | bytes 393224 | tf_op jit(solution)/shard_map/ppermute | solution.py:121
  24.4 14.8 %collective-permute-start.1 = (bf16[4,128,128]{2,1,0:T(8,128)(2,1)S(1)}, bf16[4,128,128]{2,1,0:T(8,128)(2,1)S(1)}, u32[]{:S(2)}, u32[]{:S(2)}) collective-permute-start(bf16[4,128,128]{2,1,0:T(8,128)(2,1)S(1)} %pad_maximum_fusion.2), channel_id=1, source_target_pairs={{0,3},{1,0},{2,1},{3,2},{4,7},{5,4},{6,5},{7,6},{8,11},{9,8},{10,9... | collective-permute-start | bytes 393224 | tf_op jit(solution)/shard_map/ppermute | solution.py:121
  27.9 11.9 %collective-permute-start.2 = (bf16[4,128,128]{2,1,0:T(8,128)(2,1)S(1)}, bf16[4,128,128]{2,1,0:T(8,128)(2,1)S(1)}, u32[]{:S(2)}, u32[]{:S(2)}) collective-permute-start(bf16[4,128,128]{2,1,0:T(8,128)(2,1)S(1)} %pad_maximum_fusion.2), channel_id=1, source_target_pairs={{0,2},{1,3},{2,0},{3,1},{4,6},{5,7},{6,4},{7,5},{8,10},{9,11},{10,... | collective-permute-start | bytes 393224 | tf_op jit(solution)/shard_map/ppermute | solution.py:121
  28.3 11.5 %collective-permute-start.3 = (bf16[4,128,128]{2,1,0:T(8,128)(2,1)S(1)}, bf16[4,128,128]{2,1,0:T(8,128)(2,1)S(1)}, u32[]{:S(2)}, u32[]{:S(2)}) collective-permute-start(bf16[4,128,128]{2,1,0:T(8,128)(2,1)S(1)} %pad_maximum_fusion.2), channel_id=1, source_target_pairs={{0,1},{1,2},{2,3},{3,0},{4,5},{5,6},{6,7},{7,4},{8,9},{9,10},{10,1... | collective-permute-start | bytes 393224 | tf_op jit(solution)/shard_map/ppermute | solution.py:121
  36.0 10.0 %collective-permute-start.20 = (bf16[8,128,128]{2,1,0:T(8,128)(2,1)S(1)}, bf16[8,128,128]{2,1,0:T(8,128)(2,1)S(1)}, u32[]{:S(2)}, u32[]{:S(2)}) collective-permute-start(bf16[8,128,128]{2,1,0:T(8,128)(2,1)S(1)} %get-tuple-element.31), channel_id=1, source_target_pairs={{0,24},{8,0},{16,8},{24,16},{1,25},{9,1},{17,9},{25,17},{2,26},{10... | collective-permute-start | bytes 786440 | tf_op jit(solution)/shard_map/ppermute | solution.py:121
  39.1 16.8 %collective-permute-start.18 = (bf16[8,128,128]{2,1,0:T(8,128)(2,1)S(1)}, bf16[8,128,128]{2,1,0:T(8,128)(2,1)S(1)}, u32[]{:S(2)}, u32[]{:S(2)}) collective-permute-start(bf16[8,128,128]{2,1,0:T(8,128)(2,1)S(1)} %get-tuple-element.29), channel_id=1, source_target_pairs={{0,8},{8,16},{16,24},{24,0},{1,9},{9,17},{17,25},{25,1},{2,10},{10... | collective-permute-start | bytes 786440 | tf_op jit(solution)/shard_map/ppermute | solution.py:121
  42.7 13.5 %collective-permute-start.6 = (bf16[8,128,128]{2,1,0:T(8,128)(2,1)S(1)}, bf16[8,128,128]{2,1,0:T(8,128)(2,1)S(1)}, u32[]{:S(2)}, u32[]{:S(2)}) collective-permute-start(bf16[8,128,128]{2,1,0:T(8,128)(2,1)S(1)} %get-tuple-element.23), channel_id=1, source_target_pairs={{0,24},{8,0},{16,8},{24,16},{1,25},{9,1},{17,9},{25,17},{2,26},{10... | collective-permute-start | bytes 786440 | tf_op jit(solution)/shard_map/ppermute | solution.py:121
  44.8 12.8 %collective-permute-start.5 = (bf16[8,128,128]{2,1,0:T(8,128)(2,1)S(1)}, bf16[8,128,128]{2,1,0:T(8,128)(2,1)S(1)}, u32[]{:S(2)}, u32[]{:S(2)}) collective-permute-start(bf16[8,128,128]{2,1,0:T(8,128)(2,1)S(1)} %get-tuple-element.22), channel_id=1, source_target_pairs={{0,16},{8,24},{16,0},{24,8},{1,17},{9,25},{17,1},{25,9},{2,18},{10... | collective-permute-start | bytes 786440 | tf_op jit(solution)/shard_map/ppermute | solution.py:121
  46.1 19.0 %collective-permute-start.4 = (bf16[8,128,128]{2,1,0:T(8,128)(2,1)S(1)}, bf16[8,128,128]{2,1,0:T(8,128)(2,1)S(1)}, u32[]{:S(2)}, u32[]{:S(2)}) collective-permute-start(bf16[8,128,128]{2,1,0:T(8,128)(2,1)S(1)} %get-tuple-element.21), channel_id=1, source_target_pairs={{0,8},{8,16},{16,24},{24,0},{1,9},{9,17},{17,25},{25,1},{2,10},{10... | collective-permute-start | bytes 786440 | tf_op jit(solution)/shard_map/ppermute | solution.py:121
  65.7 14.2 %collective-permute-start.23 = (bf16[8,128,128]{2,1,0:T(8,128)(2,1)S(1)}, bf16[8,128,128]{2,1,0:T(8,128)(2,1)S(1)}, u32[]{:S(2)}, u32[]{:S(2)}) collective-permute-start(bf16[8,128,128]{2,1,0:T(8,128)(2,1)S(1)} %get-tuple-element.40), channel_id=1, source_target_pairs={{0,8},{8,16},{16,24},{24,0},{1,9},{9,17},{17,25},{25,1},{2,10},{10... | collective-permute-start | bytes 786440 | tf_op jit(solution)/shard_map/ppermute | solution.py:121
  65.8 14.1 %collective-permute-start.22 = (bf16[8,128,128]{2,1,0:T(8,128)(2,1)S(1)}, bf16[8,128,128]{2,1,0:T(8,128)(2,1)S(1)}, u32[]{:S(2)}, u32[]{:S(2)}) collective-permute-start(bf16[8,128,128]{2,1,0:T(8,128)(2,1)S(1)} %get-tuple-element.40), channel_id=1, source_target_pairs={{0,16},{8,24},{16,0},{24,8},{1,17},{9,25},{17,1},{25,9},{2,18},{10... | collective-permute-start | bytes 786440 | tf_op jit(solution)/shard_map/ppermute | solution.py:121
  66.5 13.7 %collective-permute-start.21 = (bf16[8,128,128]{2,1,0:T(8,128)(2,1)S(1)}, bf16[8,128,128]{2,1,0:T(8,128)(2,1)S(1)}, u32[]{:S(2)}, u32[]{:S(2)}) collective-permute-start(bf16[8,128,128]{2,1,0:T(8,128)(2,1)S(1)} %get-tuple-element.40), channel_id=1, source_target_pairs={{0,24},{8,0},{16,8},{24,16},{1,25},{9,1},{17,9},{25,17},{2,26},{10... | collective-permute-start | bytes 786440 | tf_op jit(solution)/shard_map/ppermute | solution.py:121
  90.7 100.7 %reduce-scatter.5.cloned.1.call-start = ((), (), s32[]{:S(2)}) async-start(), calls=%async_computation.3 | async-start | bytes 2621440 | tf_op jit(solution)/shard_map/reduce_scatter | solution.py:149
  90.8 8.8 %collective-permute-start.9 = (bf16[8,128,128]{2,1,0:T(8,128)(2,1)S(1)}, bf16[8,128,128]{2,1,0:T(8,128)(2,1)S(1)}, u32[]{:S(2)}, u32[]{:S(2)}) collective-permute-start(bf16[8,128,128]{2,1,0:T(8,128)(2,1)S(1)} %get-tuple-element.41), channel_id=1, source_target_pairs={{0,8},{8,16},{16,24},{24,0},{1,9},{9,17},{17,25},{25,1},{2,10},{10... | collective-permute-start | bytes 786440 | tf_op jit(solution)/shard_map/ppermute | solution.py:121
  90.9 14.9 %collective-permute-start.8 = (bf16[8,128,128]{2,1,0:T(8,128)(2,1)S(1)}, bf16[8,128,128]{2,1,0:T(8,128)(2,1)S(1)}, u32[]{:S(2)}, u32[]{:S(2)}) collective-permute-start(bf16[8,128,128]{2,1,0:T(8,128)(2,1)S(1)} %get-tuple-element.41), channel_id=1, source_target_pairs={{0,16},{8,24},{16,0},{24,8},{1,17},{9,25},{17,1},{25,9},{2,18},{10... | collective-permute-start | bytes 786440 | tf_op jit(solution)/shard_map/ppermute | solution.py:121
  94.1 11.7 %collective-permute-start.7 = (bf16[8,128,128]{2,1,0:T(8,128)(2,1)S(1)}, bf16[8,128,128]{2,1,0:T(8,128)(2,1)S(1)}, u32[]{:S(2)}, u32[]{:S(2)}) collective-permute-start(bf16[8,128,128]{2,1,0:T(8,128)(2,1)S(1)} %get-tuple-element.41), channel_id=1, source_target_pairs={{0,24},{8,0},{16,8},{24,16},{1,25},{9,1},{17,9},{25,17},{2,26},{10... | collective-permute-start | bytes 786440 | tf_op jit(solution)/shard_map/ppermute | solution.py:121
  120.0 12.4 %collective-permute-start.12 = (bf16[4,128,128]{2,1,0:T(8,128)(2,1)S(1)}, bf16[4,128,128]{2,1,0:T(8,128)(2,1)S(1)}, u32[]{:S(2)}, u32[]{:S(2)}) collective-permute-start(bf16[4,128,128]{2,1,0:T(8,128)(2,1)S(1)} %get-tuple-element.27), channel_id=1, source_target_pairs={{0,3},{1,0},{2,1},{3,2},{4,7},{5,4},{6,5},{7,6},{8,11},{9,8},{10,9... | collective-permute-start | bytes 393224 | tf_op jit(solution)/shard_map/ppermute | solution.py:121
  120.5 12.7 %collective-permute-start.11 = (bf16[4,128,128]{2,1,0:T(8,128)(2,1)S(1)}, bf16[4,128,128]{2,1,0:T(8,128)(2,1)S(1)}, u32[]{:S(2)}, u32[]{:S(2)}) collective-permute-start(bf16[4,128,128]{2,1,0:T(8,128)(2,1)S(1)} %get-tuple-element.26), channel_id=1, source_target_pairs={{0,2},{1,3},{2,0},{3,1},{4,6},{5,7},{6,4},{7,5},{8,10},{9,11},{10,... | collective-permute-start | bytes 393224 | tf_op jit(solution)/shard_map/ppermute | solution.py:121
  121.9 11.3 %collective-permute-start.10 = (bf16[4,128,128]{2,1,0:T(8,128)(2,1)S(1)}, bf16[4,128,128]{2,1,0:T(8,128)(2,1)S(1)}, u32[]{:S(2)}, u32[]{:S(2)}) collective-permute-start(bf16[4,128,128]{2,1,0:T(8,128)(2,1)S(1)} %get-tuple-element.25), channel_id=1, source_target_pairs={{0,1},{1,2},{2,3},{3,0},{4,5},{5,6},{6,7},{7,4},{8,9},{9,10},{10,1... | collective-permute-start | bytes 393224 | tf_op jit(solution)/shard_map/ppermute | solution.py:121
  132.5 8.4 %collective-permute-start.24 = (bf16[4,128,128]{2,1,0:T(8,128)(2,1)S(1)}, bf16[4,128,128]{2,1,0:T(8,128)(2,1)S(1)}, u32[]{:S(2)}, u32[]{:S(2)}) collective-permute-start(bf16[4,128,128]{2,1,0:T(8,128)(2,1)S(1)} %get-tuple-element.33), channel_id=1, source_target_pairs={{0,1},{1,2},{2,3},{3,0},{4,5},{5,6},{6,7},{7,4},{8,9},{9,10},{10,1... | collective-permute-start | bytes 393224 | tf_op jit(solution)/shard_map/ppermute | solution.py:121
  142.0 51.2 %collective-permute-start.30 = (bf16[64,16,128]{2,1,0:T(8,128)(2,1)S(1)}, bf16[64,16,128]{2,1,0:T(8,128)(2,1)S(1)}, u32[]{:S(2)}, u32[]{:S(2)}) collective-permute-start(bf16[64,16,128]{2,1,0:T(8,128)(2,1)S(1)} %slice_bitcast_fusion.2), channel_id=1, source_target_pairs={{0,32},{32,0},{1,33},{33,1},{2,34},{34,2},{3,35},{35,3},{4,36},{36... | collective-permute-start | bytes 786440 | tf_op jit(solution)/shard_map/ppermute | solution.py:125
  (17 other events, 81.3 us)
Sparse Core Ops, SparseCore 0:
  90.9 46.1 reduce-scatter.2
  139.8 51.5 reduce-scatter.4
